TPU v7x, 256 devices: a whole 4x4x8 slice. The times are simulated.
256 devices in a mesh: grp: 16 (over x_hi, y, core), tile: 16 (over z, x_lo).
Axes of the slice: x: 4 (x_hi: 2, x_lo: 2; x = x_hi * 2 + x_lo), y: 4, z: 8, core: 2. Of those that a mesh axis runs over, the one named last changes fastest.
Arguments:
- features: float32 [16, 16, 9, 2, 8, 512], P('grp', 'tile'), may hold values from -150 to 150
- lengths: int32 [16], replicated, may hold values from 1 to 9, as said below
- offsets: int32 [16], P('tile'), may hold values from 0 to 15
- norm_gain: float32 [512], replicated, may hold values from 0.1 to 1.9
- norm_bias: float32 [512], replicated, may hold values from -3 to 3
- time_weight: float32 [3, 512, 1024], replicated, may hold values from -0.15625 to 0.15625
- time_bias: float32 [1024], replicated, may hold values from -2 to 2
- space_weight: float32 [3, 3, 512, 256], replicated, may hold values from -0.09375 to 0.09375
- space_bias: float32 [256], replicated, may hold values from -3 to 3
Outputs:
- upsampled_tiles: float32 [16, 16, 18, 4, 16, 256], P('grp', 'tile')
Inputs may be any that keep to these rules, and one draw needn't show every extreme that they name: `lengths`: at least one video has all 9 frames.
All inputs are finite; a program needn't handle non-finite values.
Results may differ from a plain program's by a relative error of at most 0.0003.
Values sent between devices are 32-bit elements; how exact they have to be, the bound alone decides.
A program may use at most 128 MiB of HBM per device.

v0:
```python
import jax
import jax.numpy as jnp
from jax import lax
from jax.experimental import pallas as pl
from jax.experimental.pallas import tpu as pltpu
from jax.sharding import PartitionSpec as P

F32, BF16 = jnp.float32, jnp.bfloat16
GROUPS = 32


def split(value):
    high = value.astype(BF16)
    return high, (value - high.astype(F32)).astype(BF16)


def prepare_time(raw, high, low):
    rows = 64
    taps, depth, width = raw.shape

    @pl.loop(0, taps * depth // rows)
    def _(step):
        tap = step // (depth // rows)
        at = pl.ds(pl.multiple_of(step % (depth // rows) * rows, rows), rows)
        high[tap, at], low[tap, at] = split(raw[tap, at])


def prepare_space(raw, high, low):
    rows = 32
    depth = raw.shape[2]

    @pl.loop(0, depth // rows)
    def _(step):
        at = pl.ds(pl.multiple_of(step * rows, rows), rows)
        kernel = [[raw[a, b, at] for b in range(3)] for a in range(3)]
        by_row = [kernel[0], [kernel[0][b] + kernel[1][b] + kernel[2][b] for b in range(3)], kernel[2]]
        for a in range(3):
            one = by_row[a]
            for b, value in enumerate((one[0], one[0] + one[1] + one[2], one[2])):
                high[a * 3 + b, at], low[a * 3 + b, at] = split(value)


def dots(pairs):
    total = None
    for left, right in pairs:
        part = jnp.dot(left, right, preferred_element_type=F32)
        total = part if total is None else total + part
    return total


def normalize(frames, first, block, mean, scale, gain, bias, act_high, act_low):
    for step in range(frames):
        value = block[first + step]
        inner = (value - mean) * scale * gain + bias
        inner = inner / (1.0 + jnp.exp(-inner))
        act_high[first + step + 2], act_low[first + step + 2] = split(inner)


def decode(frames, first, keep, upper, has_left, has_right, act, time, time_bias, space, space_bias, temporal, ops, out):
    (act_high, act_low), (time_high, time_low), (space_high, space_low), (op_high, op_low) = act, time, space, ops
    rows = frames * 32
    depth = act_high.shape[-1]
    pairs = []
    for tap in range(3):
        high = act_high[pl.ds(first + tap, frames)].reshape(rows, depth)
        low = act_low[pl.ds(first + tap, frames)].reshape(rows, depth)
        pairs += [(high, time_high[tap]), (low, time_high[tap]), (high, time_low[tap])]
    temporal[...] = dots(pairs) + time_bias[...]
    place = lax.broadcasted_iota(jnp.int32, (8, depth), 0)
    for frame in range(frames):
        for half in range(2):
            lanes = slice(half * depth, half * depth + depth)
            block = lambda i: temporal[frame * 32 + i * 8:frame * 32 + i * 8 + 8, lanes]
            row0, row1, across, side = block(0), block(1), block(2), block(3)
            columns = []
            for row, left, right in ((row0, 0, 2), (row1, 1, 3), (across, 4, 5)):
                before = jnp.where(place == 0, side[left:left + 1] * has_left, pltpu.roll(row, 1, 0))
                after = jnp.where(place == 7, side[right:right + 1] * has_right, pltpu.roll(row, 7, 0))
                columns.append((before - row, row, after - row))
            start = (frame * 2 + half) * 16
            for b in range(3):
                row0, row1, across = columns[0][b], columns[1][b], columns[2][b]
                above = across * (1.0 - upper)
                below = across * upper
                for a, value in enumerate((
                    jnp.concatenate([above - row0, row0 - row1], axis=0),
                    jnp.concatenate([row0, row1], axis=0),
                    jnp.concatenate([row1 - row0, below - row1], axis=0),
                )):
                    op_high[a * 3 + b, start:start + 16], op_low[a * 3 + b, start:start + 16] = split(value)
    parts = []
    for k in range(9):
        high, low = op_high[k], op_low[k]
        parts.append(dots([(high, space_high[k]), (low, space_high[k]), (high, space_low[k])]))
    for up in range(2):
        base = parts[3 * (2 * up)], parts[3 * (2 * up) + 1], parts[3 * (2 * up) + 2]
        base = [base[b] + parts[3 + b] for b in range(3)]
        for side in range(2):
            value = base[1] + base[2 * side] + space_bias[...]
            for frame in range(frames):
                for half in range(2):
                    start = (frame * 2 + half) * 16
                    valid = (first + frame) < keep
                    for row in range(2):
                        piece = value[start + row * 8:start + row * 8 + 8]
                        piece = jnp.where(valid, piece, 0.0)
                        for lane in range(2):
                            out[lane, (first + frame) * 2 + half, row * 2 + up, pl.ds(side, 8, stride=2), :] = piece[:, lane * 128:lane * 128 + 128]


MESH = pl.DeviceIdType.MESH
ACROSS, RIGHT, LEFT, ACROSS_RIGHT, ACROSS_LEFT = range(5)
MIRROR = (ACROSS, LEFT, RIGHT, ACROSS_LEFT, ACROSS_RIGHT)
SIDES = (RIGHT, RIGHT, LEFT, LEFT, ACROSS_RIGHT, ACROSS_LEFT)
PIECES = ((0, 8, 16), (8, 2, 24), (10, 2, 26), (12, 1, 28), (13, 1, 29))
SENT = 32


def wide(value, times=4):
    return jnp.concatenate([value] * times, axis=-1)


def group_sums(value):
    lane = lax.broadcasted_iota(jnp.int32, value.shape, 1)
    for step in (1, 2, 4, 8):
        ahead, behind = pltpu.roll(value, 128 - step, 1), pltpu.roll(value, step, 1)
        value = value + jnp.where(lane & step == 0, ahead, behind)
    return value


def tile_neighbours(tile):
    column, row = tile % 8, tile // 8
    right, left = (column + 1) % 8, (column + 7) % 8
    own, other = row * 8, (1 - row) * 8
    return other + column, own + right, own + left, other + right, other + left


def gather_kernel(
    offsets, lengths, features, block, stats,
    near, swap_out, swap_in, core_out, core_in, halo, marks, mark_in, kinds, sums, sums_in, norms, norms_in,
    near_sem, swap_sem, core_sem, halo_sem, mark_sem, sums_sem, norms_sem,
):
    frames = features.shape[0]
    grp, tile = lax.axis_index("grp"), lax.axis_index("tile")
    neighbours = tile_neighbours(tile)
    facing = 1 - tile // 8

    def send(source, target, sems, at, device):
        out_sem, in_sem = sems
        return pltpu.make_async_remote_copy(
            src_ref=source, dst_ref=target, send_sem=out_sem.at[at], recv_sem=in_sem.at[at],
            device_id=device, device_id_type=MESH,
        )

    def near_copy(step, frame):
        return send(features.at[frame], near.at[step - 1, frame], near_sem, (step - 1, frame), (grp ^ (step * 2), tile))

    def swap_copy(frame):
        rows = pl.ds(0, SENT)
        return send(swap_out.at[frame, rows], swap_in.at[frame, rows], swap_sem, frame, (grp ^ 8, tile))

    def core_copy(frame):
        rows = pl.ds(0, SENT)
        return send(core_out.at[frame, rows], core_in.at[frame, rows], core_sem, frame, (grp ^ 1, tile))

    def halo_copy(kind, frame):
        start, count, land = PIECES[kind]
        return send(
            halo.at[frame, pl.ds(start, count)], block.at[frame, pl.ds(land, count)],
            halo_sem, (kind, frame), (grp, neighbours[kind]),
        )

    def mark_copy(kind):
        return send(marks, mark_in.at[MIRROR[kind]], mark_sem, MIRROR[kind], (grp, neighbours[kind]))

    def sums_copy(step):
        return send(sums, sums_in.at[step], sums_sem, step, (grp, (tile + step) % 16))

    def norms_copy(step):
        return send(norms, norms_in.at[step], norms_sem, step, (grp ^ step, tile))

    block[:, 24:32] = jnp.zeros((frames, 8, 512), F32)
    barrier = pltpu.get_barrier_semaphore()

    @pl.loop(1, 16)
    def _(step):
        pl.semaphore_signal(barrier, inc=1, device_id=(grp, (tile + step) % 16), device_id_type=MESH)
        pl.semaphore_signal(barrier, inc=1, device_id=(grp ^ step, tile), device_id_type=MESH)

    marks[...] = jnp.full(marks.shape, offsets[0], jnp.int32)
    length = lengths[grp]
    total, squares = jnp.zeros((8, 512), F32), jnp.zeros((8, 512), F32)
    for frame in range(frames):
        for row in range(2):
            value = jnp.where(frame < length, features[frame, row * 8 : row * 8 + 8], 0.0)
            total, squares = total + value, squares + value * value
    total, squares = jnp.sum(total, axis=0, keepdims=True), jnp.sum(squares, axis=0, keepdims=True)
    for part in range(4):
        sums[part : part + 1] = total[:, part * 128 : part * 128 + 128]
        sums[part + 4 : part + 5] = squares[:, part * 128 : part * 128 + 128]

    pl.semaphore_wait(barrier, 30)
    for kind in range(5):
        mark_copy(kind).start()

    @pl.loop(1, 16)
    def _(step):
        sums_copy(step).start()

    @pl.loop(0, frames)
    def _(frame):
        for step in (1, 2, 3):
            near_copy(step, frame).start()

    swap_out[:, 24:32] = jnp.zeros((frames, 8, 512), F32)

    for kind in range(5):
        mark_copy(kind).wait_recv()
    kinds[0] = marks[...]
    kinds[1] = mark_in[ACROSS]
    kinds[2] = jnp.concatenate([mark_in[kind][0:1] for kind in SIDES] + [marks[0:2]], axis=0)

    def chosen(rows, frame, mark):
        pick = wide(mark // 2 % 4)
        value = features[frame, rows]
        for step in (1, 2, 3):
            value = jnp.where(pick == step, near[step - 1, frame, rows], value)
        return value

    def start_swap(frame):
        for step in (1, 2, 3):
            near_copy(step, frame).wait_recv()
        for row in range(2):
            swap_out[frame, row * 8 : row * 8 + 8] = chosen(pl.ds(row * 8, 8), frame, kinds[0])
        swap_out[frame, 16:24] = chosen(pl.ds(pl.multiple_of(facing * 8, 8), 8), frame, kinds[1])
        for place, source in enumerate((7, 15, 0, 8, facing * 8 + 7, facing * 8)):
            mark = kinds[2, place : place + 1]
            swap_out[frame, 24 + place : 25 + place] = chosen(pl.ds(source, 1), frame, mark)
        swap_copy(frame).start()

    def start_core(frame):
        swap_copy(frame).wait_recv()
        for part, kind in enumerate((0, 0, 1, 2)):
            rows = slice(part * 8, part * 8 + 8)
            crossed = wide(kinds[kind]) // 8 == 1
            core_out[frame, rows] = jnp.where(crossed, swap_in[frame, rows], swap_out[frame, rows])
        core_copy(frame).start()

    def start_halo(frame):
        core_copy(frame).wait_recv()
        for part, kind in enumerate((0, 0, 1, 2)):
            rows = slice(part * 8, part * 8 + 8)
            crossed = wide(kinds[kind]) % 2 == 1
            value = jnp.where(crossed, core_in[frame, rows], core_out[frame, rows])
            if part < 2:
                block[frame, rows] = value
            else:
                halo[frame, part * 8 - 16 : part * 8 - 8] = value
        for kind in range(5):
            halo_copy(kind, frame).start()

    @pl.loop(0, frames + 3)
    def _(step):
        @pl.when(step < frames)
        def _():
            start_swap(step)

        @pl.when((step >= 1) & (step < frames + 1))
        def _():
            start_core(step - 1)

        @pl.when((step >= 2) & (step < frames + 2))
        def _():
            start_halo(step - 2)

        @pl.when(step == 1)
        def _():
            @pl.loop(1, 16)
            def _(other):
                sums_copy(other).wait_recv()

            value = sums[...]
            for other in range(1, 16):
                value = value + sums_in[other]
            value = group_sums(value) / (length.astype(F32) * 4096.0)
            mean = value[0:4]
            norms[0:4] = mean
            norms[4:8] = 1.0 / jnp.sqrt(value[4:8] - mean * mean + 1e-6)

            @pl.loop(1, 16)
            def _(other):
                norms_copy(other).start()

        @pl.when(step >= 3)
        def _():
            for kind in range(5):
                halo_copy(kind, step - 3).wait_recv()

    @pl.loop(1, 16)
    def _(other):
        norms_copy(other).wait_recv()

    value = norms[...]
    for other in range(1, 16):
        value = jnp.where(marks[...] == other, norms_in[other], value)
    stats[...] = value

    for kind in range(5):
        mark_copy(kind).wait_send()

    @pl.loop(1, 16)
    def _(other):
        sums_copy(other).wait_send()
        norms_copy(other).wait_send()

    @pl.loop(0, frames)
    def _(frame):
        for step in (1, 2, 3):
            near_copy(step, frame).wait_send()
        swap_copy(frame).wait_send()
        core_copy(frame).wait_send()
        for kind in range(5):
            halo_copy(kind, frame).wait_send()


def gathered(offsets, lengths, features):
    frames = features.shape[0]
    whole, scalars = pl.BlockSpec(memory_space=pltpu.VMEM), pl.BlockSpec(memory_space=pltpu.SMEM)
    sems = lambda *shape: [[pltpu.SemaphoreType.DMA(shape)] * 2]
    buffer = lambda *shape: pltpu.VMEM(shape, F32)
    return pl.pallas_call(
        gather_kernel,
        out_shape=(jax.ShapeDtypeStruct((frames, 32, 512), F32), jax.ShapeDtypeStruct((8, 128), F32)),
        in_specs=[scalars, scalars, whole],
        out_specs=(whole, whole),
        scratch_shapes=[buffer(3, frames, 16, 512)]
        + [buffer(frames, 32, 512)] * 4
        + [buffer(frames, 16, 512)]
        + [pltpu.VMEM(shape, jnp.int32) for shape in ((8, 128), (5, 8, 128), (3, 8, 128))]
        + [buffer(8, 128), buffer(16, 8, 128)] * 2
        + sems(3, frames) + sems(frames) * 2 + sems(5, frames) + sems(5) + sems(16) * 2,
        compiler_params=pltpu.CompilerParams(
            collective_id=0, has_side_effects=True, vmem_limit_bytes=40 * 2**20
        ),
    )(offsets, lengths, features)


def decode_kernel(keep, block, stats, gain, bias, time_raw, time_bias, space_raw, space_bias, result,
                  time_f32, space_f32, time_high, time_low, space_high, space_low, act_high, act_low,
                  temporal, op_high, op_low, out, sem):
    frames = block.shape[0]
    tile = lax.axis_index("tile")
    copies = [pltpu.make_async_copy(time_raw, time_f32, sem.at[0]), pltpu.make_async_copy(space_raw, space_f32, sem.at[1])]
    for copy in copies:
        copy.start()
    act_high[0:2] = jnp.zeros((2, 32, 512), BF16)
    act_low[0:2] = jnp.zeros((2, 32, 512), BF16)
    lanes = lambda row: jnp.concatenate([stats[row + i : row + i + 1] for i in range(4)], axis=1)
    mean, scale = lanes(0), lanes(4)
    normalize(frames, 0, block, mean, scale, gain[...], bias[...], act_high, act_low)
    copies[0].wait()
    prepare_time(time_f32, time_high, time_low)
    copies[1].wait()
    prepare_space(space_f32, space_high, space_low)
    number = lambda flag: flag.astype(F32)
    decode(
        frames, 0, keep[0], number(tile < 8), number(tile % 8 != 0), number(tile % 8 != 7),
        (act_high, act_low), (time_high, time_low), time_bias, (space_high, space_low), space_bias,
        temporal, (op_high, op_low), out,
    )
    copies = [
        pltpu.make_async_copy(out.at[lane], result.at[:, :, :, pl.ds(lane * 128, 128)], sem.at[lane]) for lane in range(2)
    ]
    for copy in copies:
        copy.start()
    for copy in copies:
        copy.wait()


def decoded(keep, block, stats, gain, bias, time_weight, time_bias, space_weight, space_bias):
    frames = block.shape[0]
    whole, scalars, anywhere = (pl.BlockSpec(memory_space=kind) for kind in (pltpu.VMEM, pltpu.SMEM, pl.ANY))
    buffer = lambda kind, *shape: pltpu.VMEM(shape, kind)
    return pl.pallas_call(
        decode_kernel,
        out_shape=jax.ShapeDtypeStruct((2 * frames, 4, 16, 256), F32),
        in_specs=[scalars, whole, whole, whole, whole, anywhere, whole, anywhere, whole],
        out_specs=anywhere,
        scratch_shapes=[buffer(F32, 3, 512, 1024), buffer(F32, 3, 3, 512, 256)]
        + [buffer(BF16, 3, 512, 1024)] * 2
        + [buffer(BF16, 9, 512, 256)] * 2
        + [buffer(BF16, frames + 2, 32, 512)] * 2
        + [buffer(F32, frames * 32, 1024)]
        + [buffer(BF16, 9, frames * 32, 512)] * 2
        + [buffer(F32, 2, 2 * frames, 4, 16, 128), pltpu.SemaphoreType.DMA((2,))],
        compiler_params=pltpu.CompilerParams(vmem_limit_bytes=52 * 2**20),
    )(keep, block, stats, gain, bias, time_weight, time_bias, space_weight, space_bias)


def on_device(features, lengths, offsets, norm_gain, norm_bias, time_weight, time_bias, space_weight, space_bias):
    frames, channels = features.shape[2], features.shape[-1]
    source = lax.axis_index("grp") ^ offsets[0]
    block, stats = gathered(offsets, lengths, features.reshape(frames, 16, channels))
    row = lambda array: array.reshape(1, -1)
    result = decoded(
        lengths[source][None], block, stats, row(norm_gain), row(norm_bias),
        time_weight, row(time_bias), space_weight, row(space_bias),
    )
    return result[None, None]


def solution(mesh):
    in_specs = (P("grp", "tile", None, None, None, None), P(), P("tile"), P(), P(), P(), P(), P(), P())
    out_specs = P("grp", "tile", None, None, None, None)
    return jax.shard_map(on_device, mesh=mesh, in_specs=in_specs, out_specs=out_specs, check_vma=False)
```

profile of v0, /device:TPU:8, one launch (start us, length us, event | category | flops | bytes accessed | tf_op | source)
XLA Modules:
  0.0 73.5 jit_solution(18403014842101999349)
XLA Ops:
  0.7 1.3 %dynamic_slice.3.keep = s32[1]{0:T(128)} dynamic-slice(s32[16]{0:T(128)} %lengths.1, s32[]{:T(128)S(6)} %select_n.3), dynamic_slice_sizes={1} | dynamic-slice | bytes 12 | tf_op jit(solution)/shard_map/dynamic_slice | solution.py:406
  2.0 0.0 copy-start
  2.0 1.0 %copy-done = f32[1,1,9,2,8,512]{5,4,3,2,1,0:T(8,128)S(1)} copy-done((f32[1,1,9,2,8,512]{5,4,3,2,1,0:T(8,128)S(1)}, f32[1,1,9,2,8,512]{5,4,3,2,1,0:T(8,128)}, u32[]{:S(2)}) %copy-start) | copy-done | bytes 294936
  2.9 0.0 copy-start.5
  2.9 0.7 copy-done.5
  3.6 54.9 %shard_map.91 = (f32[9,32,512]{2,1,0:T(8,128)S(1)}, f32[8,128]{1,0:T(8,128)S(1)}) custom-call(s32[1]{0:T(128)} %copy.10.offsets, s32[16]{0:T(128)S(1)} %copy-done.5, f32[9,16,512]{2,1,0:T(8,128)S(1)} %bitcast.8), custom_call_target="tpu_custom_call" | custom-call | tf_op jit(solution)/shard_map/pallas_call | solution.py:331
  58.5 0.0 copy-start.1
  58.6 0.7 copy-done.1
  59.2 0.0 copy-start.2
  59.2 0.7 copy-done.2
  59.9 0.0 copy-start.3
  59.9 0.7 copy-done.3
  60.6 0.0 copy-start.4
  60.6 0.7 copy-done.4
  61.3 12.2 %shard_map.92 = f32[18,4,16,256]{3,2,1,0:T(8,128)} custom-call(s32[1]{0:T(128)} %dynamic_slice.3.keep, f32[9,32,512]{2,1,0:T(8,128)S(1)} %get-tuple-element.7.block, f32[8,128]{1,0:T(8,128)S(1)} %get-tuple-element.8.stats, f32[1,512]{1,0:T(1,128)S(1)} %bitcast.10, f32[1,512]{1,0:T(1,128)S(1)} %bitcast.11, f32[3,512,1024]{2,1,0:T(8,128)} %time_raw.1, ...), custom_call_target="tpu_custom_call" | custom-call | tf_op jit(solution)/shard_map/pallas_call | solution.py:384
Async XLA Ops:
  2.0 1.0 %copy-start = (f32[1,1,9,2,8,512]{5,4,3,2,1,0:T(8,128)S(1)}, f32[1,1,9,2,8,512]{5,4,3,2,1,0:T(8,128)}, u32[]{:S(2)}) copy-start(f32[1,1,9,2,8,512]{5,4,3,2,1,0:T(8,128)} %param.9) | copy-start | bytes 884740
  2.9 0.7 copy-start.5
  58.5 0.7 copy-start.1
  59.2 0.7 copy-start.2
  59.9 0.7 copy-start.3
  60.6 0.7 copy-start.4
where the time goes:
time: 73.7 us; the launch traced here: 73.5 us
  Pallas kernels  67.2 us (91%)
  local copies, waits for them, and re-layouts  5.66 us (8%)
    pallas_call x1, Pallas kernels, gathered(): pl.pallas_call(gather_kernel, out_shape=(jax.ShapeDtypeStruct((frames, 32...  54.9 us
    pallas_call x1, Pallas kernels, decoded(): pl.pallas_call(decode_kernel, out_shape=jax.ShapeDtypeStruct((2 * frames,...  12.2 us
    unnamed x12, local copies, waits for them, and re-layouts  4.34 us

commit v1 on v0

v1 whole, which is shorter than its diff:
```python
import jax
import jax.numpy as jnp
from jax import lax
from jax.experimental import pallas as pl
from jax.experimental.pallas import tpu as pltpu
from jax.sharding import PartitionSpec as P

F32, BF16 = jnp.float32, jnp.bfloat16


def split(value):
    high = value.astype(BF16)
    return high, (value - high.astype(F32)).astype(BF16)


def prepare_time(step, raw, both):
    rows = 64
    depth = raw.shape[1]
    tap = step // (depth // rows)
    at = pl.ds(pl.multiple_of(step % (depth // rows) * rows, rows), rows)
    both[0, tap, at], both[1, tap, at] = split(raw[tap, at])


def prepare_space(step, raw, both):
    rows = 32
    at = pl.ds(pl.multiple_of(step * rows, rows), rows)
    kernel = [[raw[a, b, at] for b in range(3)] for a in range(3)]
    by_row = [kernel[0], [kernel[0][b] + kernel[1][b] + kernel[2][b] for b in range(3)], kernel[2]]
    for a in range(3):
        one = by_row[a]
        for b, value in enumerate((one[0], one[0] + one[1] + one[2], one[2])):
            both[0, a * 3 + b, at], both[1, a * 3 + b, at] = split(value)


def normalize(first, count, block, mean, scale, gain, bias, act):
    for frame in range(first, first + count):
        inner = (block[frame] - mean) * scale * gain + bias
        inner = inner / (1.0 + jnp.exp(-inner))
        act[0, frame + 2], act[1, frame + 2] = split(inner)


def decode(first, frames, keep, upper, has_left, has_right, act, time, time_bias, space, space_bias, temporal, ops, stage, out):
    rows, depth = frames * 32, act.shape[-1]
    both, high = [], []
    for tap in range(3):
        at = pl.ds(first + tap, frames)
        both.append(act[:, at].reshape(2 * rows, depth))
        high.append(act[0, at].reshape(rows, depth))
    weights = time.reshape(2, 3 * depth, 2 * depth)
    product = jnp.dot(jnp.concatenate(both, axis=1), weights[0], preferred_element_type=F32)
    yield
    rest = jnp.dot(jnp.concatenate(high, axis=1), weights[1], preferred_element_type=F32)
    temporal[0:rows] = product[:rows] + product[rows:] + rest + time_bias[...]
    yield
    place = lax.broadcasted_iota(jnp.int32, (8, depth), 0)
    for frame in range(frames):
        for half in range(2):
            lanes = slice(half * depth, half * depth + depth)
            block = lambda i: temporal[frame * 32 + i * 8 : frame * 32 + i * 8 + 8, lanes]
            row0, row1, across, side = block(0), block(1), block(2), block(3)
            columns = []
            for row, left, right in ((row0, 0, 2), (row1, 1, 3), (across, 4, 5)):
                before = jnp.where(place == 0, side[left : left + 1] * has_left, pltpu.roll(row, 1, 0))
                after = jnp.where(place == 7, side[right : right + 1] * has_right, pltpu.roll(row, 7, 0))
                columns.append((before - row, row, after - row))
            start = (frame * 2 + half) * 16
            for b in range(3):
                row0, row1, across = columns[0][b], columns[1][b], columns[2][b]
                above, below = across * (1.0 - upper), across * upper
                for a, value in enumerate((
                    jnp.concatenate([above - row0, row0 - row1], axis=0),
                    jnp.concatenate([row0, row1], axis=0),
                    jnp.concatenate([row1 - row0, below - row1], axis=0),
                )):
                    at = pl.ds(start, 16)
                    ops[a * 3 + b, 0, at], ops[a * 3 + b, 1, at] = split(value)
        yield
    parts = []
    for k in range(9):
        product = jnp.dot(ops[k, :, 0:rows].reshape(2 * rows, depth), space[0, k], preferred_element_type=F32)
        product = product[:rows] + product[rows:]
        parts.append(product + jnp.dot(ops[k, 0, 0:rows], space[1, k], preferred_element_type=F32))
        if k % 3 == 2:
            yield
    for up in range(2):
        base = [parts[6 * up + b] + parts[3 + b] for b in range(3)]
        for side in range(2):
            value = base[1] + base[2 * side] + space_bias[...]
            for frame in range(frames):
                for half in range(2):
                    start = (frame * 2 + half) * 16
                    for row in range(2):
                        piece = value[start + row * 8 : start + row * 8 + 8]
                        for lane in range(2):
                            stage[lane, frame * 2 + half, row * 2 + up, pl.ds(side, 8, stride=2), :] = piece[:, lane * 128 : lane * 128 + 128]
    yield
    for frame in range(frames):
        valid = (first + frame) < keep
        for half in range(2):
            for row in range(4):
                piece = jnp.concatenate([stage[lane, frame * 2 + half, row] for lane in range(2)], axis=1)
                out[(first + frame) * 2 + half, row] = jnp.where(valid, piece, 0.0)
    yield


MESH = pl.DeviceIdType.MESH
ACROSS, RIGHT, LEFT, ACROSS_RIGHT, ACROSS_LEFT = range(5)
MIRROR = (ACROSS, LEFT, RIGHT, ACROSS_LEFT, ACROSS_RIGHT)
SIDES = (RIGHT, RIGHT, LEFT, LEFT, ACROSS_RIGHT, ACROSS_LEFT)
PIECES = ((0, 8, 16), (8, 2, 24), (10, 2, 26), (12, 1, 28), (13, 1, 29))
SENT = 32


def wide(value, times=4):
    return jnp.concatenate([value] * times, axis=-1)


def group_sums(value):
    lane = lax.broadcasted_iota(jnp.int32, value.shape, 1)
    for step in (1, 2, 4, 8):
        ahead, behind = pltpu.roll(value, 128 - step, 1), pltpu.roll(value, step, 1)
        value = value + jnp.where(lane & step == 0, ahead, behind)
    return value


def tile_neighbours(tile):
    column, row = tile % 8, tile // 8
    right, left = (column + 1) % 8, (column + 7) % 8
    own, other = row * 8, (1 - row) * 8
    return other + column, own + right, own + left, other + right, other + left


CORE_AFTER, HALO_AFTER = 2, 3
CHUNKS = (3, 3, 3)
LOOPED = 8


def kernel(
    offsets, lengths, raw_features, gain_in, bias_in, time_in, time_bias_in, space_in, space_bias_in, result,
    features, gain, bias, time_raw, time_bias, space_raw, space_bias,
    near, swap_out, swap_in, core_out, core_in, halo, block,
    marks, mark_in, kinds, sums, sums_in, norms, norms_in,
    time, space, act, temporal, ops, stage, out,
    near_sem, swap_sem, core_sem, halo_sem, mark_sem, sums_sem, norms_sem, load_sem, store_sem,
):
    frames = features.shape[0]
    grp, tile = lax.axis_index("grp"), lax.axis_index("tile")
    neighbours = tile_neighbours(tile)
    facing = 1 - tile // 8

    loads = [
        pltpu.make_async_copy(source, target, load_sem.at[at])
        for at, (source, target) in enumerate((
            (raw_features, features), (time_in, time_raw), (space_in, space_raw), (gain_in, gain),
            (bias_in, bias), (time_bias_in, time_bias), (space_bias_in, space_bias),
        ))
    ]
    for load in loads:
        load.start()

    def send(source, target, sems, at, device):
        out_sem, in_sem = sems
        return pltpu.make_async_remote_copy(
            src_ref=source, dst_ref=target, send_sem=out_sem.at[at], recv_sem=in_sem.at[at],
            device_id=device, device_id_type=MESH,
        )

    def near_copy(step, frame):
        return send(raw_features.at[frame], near.at[step - 1, frame], near_sem, (step - 1, frame), (grp ^ (step * 2), tile))

    def swap_copy(frame):
        rows = pl.ds(0, SENT)
        return send(swap_out.at[frame, rows], swap_in.at[frame, rows], swap_sem, frame, (grp ^ 8, tile))

    def core_copy(frame):
        rows = pl.ds(0, SENT)
        return send(core_out.at[frame, rows], core_in.at[frame, rows], core_sem, frame, (grp ^ 1, tile))

    def halo_copy(kind, frame):
        start, count, land = PIECES[kind]
        return send(
            halo.at[frame, pl.ds(start, count)], block.at[frame, pl.ds(land, count)],
            halo_sem, (kind, frame), (grp, neighbours[kind]),
        )

    def mark_copy(kind):
        return send(marks, mark_in.at[MIRROR[kind]], mark_sem, MIRROR[kind], (grp, neighbours[kind]))

    def sums_copy(step):
        return send(sums, sums_in.at[step], sums_sem, step, (grp, (tile + step) % 16))

    def norms_copy(step):
        return send(norms, norms_in.at[step], norms_sem, step, (grp ^ step, tile))

    block[:, 24:32] = jnp.zeros((frames, 8, 512), F32)
    barrier = pltpu.get_barrier_semaphore()

    @pl.loop(1, 16)
    def _(step):
        pl.semaphore_signal(barrier, inc=1, device_id=(grp, (tile + step) % 16), device_id_type=MESH)
        pl.semaphore_signal(barrier, inc=1, device_id=(grp ^ step, tile), device_id_type=MESH)

    marks[...] = jnp.full(marks.shape, offsets[0], jnp.int32)
    swap_out[:, 24:32] = jnp.zeros((frames, 8, 512), F32)
    act[:, 0:2] = jnp.zeros((2, 2, 32, 512), BF16)
    length = lengths[grp]
    loads[0].wait()
    total, squares = jnp.zeros((8, 512), F32), jnp.zeros((8, 512), F32)
    for frame in range(frames):
        for row in range(2):
            value = jnp.where(frame < length, features[frame, row * 8 : row * 8 + 8], 0.0)
            total, squares = total + value, squares + value * value
    total, squares = jnp.sum(total, axis=0, keepdims=True), jnp.sum(squares, axis=0, keepdims=True)
    for part in range(4):
        sums[part : part + 1] = total[:, part * 128 : part * 128 + 128]
        sums[part + 4 : part + 5] = squares[:, part * 128 : part * 128 + 128]

    pl.semaphore_wait(barrier, 30)
    for kind in range(5):
        mark_copy(kind).start()

    @pl.loop(1, 16)
    def _(step):
        sums_copy(step).start()

    @pl.loop(0, frames)
    def _(frame):
        for step in (1, 2, 3):
            near_copy(step, frame).start()

    for kind in range(5):
        mark_copy(kind).wait_recv()
    kinds[0] = marks[...]
    kinds[1] = mark_in[ACROSS]
    kinds[2] = jnp.concatenate([mark_in[kind][0:1] for kind in SIDES] + [marks[0:2]], axis=0)

    def chosen(rows, frame, mark):
        pick = wide(mark // 2 % 4)
        value = features[frame, rows]
        for step in (1, 2, 3):
            value = jnp.where(pick == step, near[step - 1, frame, rows], value)
        return value

    def start_swap(frame):
        for step in (1, 2, 3):
            near_copy(step, frame).wait_recv()
        for row in range(2):
            swap_out[frame, row * 8 : row * 8 + 8] = chosen(pl.ds(row * 8, 8), frame, kinds[0])
        swap_out[frame, 16:24] = chosen(pl.ds(pl.multiple_of(facing * 8, 8), 8), frame, kinds[1])
        for place, source in enumerate((7, 15, 0, 8, facing * 8 + 7, facing * 8)):
            mark = kinds[2, place : place + 1]
            swap_out[frame, 24 + place : 25 + place] = chosen(pl.ds(source, 1), frame, mark)
        swap_copy(frame).start()

    def start_core(frame):
        swap_copy(frame).wait_recv()
        for part, kind in enumerate((0, 0, 1, 2)):
            rows = slice(part * 8, part * 8 + 8)
            crossed = wide(kinds[kind]) // 8 == 1
            core_out[frame, rows] = jnp.where(crossed, swap_in[frame, rows], swap_out[frame, rows])
        core_copy(frame).start()

    def start_halo(frame):
        core_copy(frame).wait_recv()
        for part, kind in enumerate((0, 0, 1, 2)):
            rows = slice(part * 8, part * 8 + 8)
            crossed = wide(kinds[kind]) % 2 == 1
            value = jnp.where(crossed, core_in[frame, rows], core_out[frame, rows])
            if part < 2:
                block[frame, rows] = value
            else:
                halo[frame, part * 8 - 16 : part * 8 - 8] = value
        for kind in range(5):
            halo_copy(kind, frame).start()

    def start_norms():
        @pl.loop(1, 16)
        def _(other):
            sums_copy(other).wait_recv()

        value = sums[...]
        for other in range(1, 16):
            value = value + sums_in[other]
        value = group_sums(value) / (length.astype(F32) * 4096.0)
        mean = value[0:4]
        norms[0:4] = mean
        norms[4:8] = 1.0 / jnp.sqrt(value[4:8] - mean * mean + 1e-6)

        @pl.loop(1, 16)
        def _(other):
            norms_copy(other).start()

    @pl.loop(0, LOOPED)
    def _(step):
        start_swap(step)

        @pl.when(step >= CORE_AFTER)
        def _():
            start_core(step - CORE_AFTER)

        @pl.when(step >= HALO_AFTER)
        def _():
            start_halo(step - HALO_AFTER)

        @pl.when(step == 0)
        def _():
            loads[1].wait()
            loads[2].wait()

        @pl.when(step < 4)
        def _():
            @pl.loop(0, 6)
            def _(piece):
                prepare_time(step * 6 + piece, time_raw, time)

            @pl.loop(0, 4)
            def _(piece):
                prepare_space(step * 4 + piece, space_raw, space)

        @pl.when(step == 1)
        def _():
            start_norms()

    @pl.loop(1, 16)
    def _(other):
        norms_copy(other).wait_recv()

    for load in loads[3:]:
        load.wait()
    value = norms[...]
    for other in range(1, 16):
        value = jnp.where(marks[...] == other, norms_in[other], value)
    mean, scale = (
        jnp.concatenate([value[row + i : row + i + 1] for i in range(4)], axis=1) for row in (0, 4)
    )
    number = lambda flag: flag.astype(F32)
    upper, has_left, has_right = number(tile < 8), number(tile % 8 != 0), number(tile % 8 != 7)
    keep = lengths[grp ^ offsets[0]]

    def store(first, count):
        rows = pl.ds(first * 2, count * 2)
        return pltpu.make_async_copy(out.at[rows], result.at[rows], store_sem.at[first])

    def compute():
        first = 0
        for count in CHUNKS:
            for frame in range(first, first + count):
                for kind in range(5):
                    halo_copy(kind, frame).wait_recv()
            normalize(first, count, block, mean, scale, gain[...], bias[...], act)
            yield
            yield from decode(
                first, count, keep, upper, has_left, has_right, act, time, time_bias, space, space_bias,
                temporal, ops, stage, out,
            )
            store(first, count).start()
            first += count

    def transfers():
        for step in range(LOOPED, frames + HALO_AFTER):
            if step < frames:
                start_swap(step)
                yield
            if step < frames + CORE_AFTER:
                start_core(step - CORE_AFTER)
                yield
            start_halo(step - HALO_AFTER)
            yield

    work, moves = compute(), transfers()
    for _ in moves:
        next(work, None)
    for _ in work:
        pass

    first = 0
    for count in CHUNKS:
        store(first, count).wait()
        first += count
    for kind in range(5):
        mark_copy(kind).wait_send()

    @pl.loop(1, 16)
    def _(other):
        sums_copy(other).wait_send()
        norms_copy(other).wait_send()

    @pl.loop(0, frames)
    def _(frame):
        for step in (1, 2, 3):
            near_copy(step, frame).wait_send()
        swap_copy(frame).wait_send()
        core_copy(frame).wait_send()
        for kind in range(5):
            halo_copy(kind, frame).wait_send()


def decoded(offsets, lengths, features, gain, bias, time_weight, time_bias, space_weight, space_bias):
    frames = features.shape[0]
    scalars, anywhere = pl.BlockSpec(memory_space=pltpu.SMEM), pl.BlockSpec(memory_space=pl.ANY)
    sems = lambda *shape: [[pltpu.SemaphoreType.DMA(shape)] * 2]
    buffer = lambda *shape, kind=F32: pltpu.VMEM(shape, kind)
    most = max(CHUNKS)
    arrays = (features, gain, bias, time_weight, time_bias, space_weight, space_bias)
    return pl.pallas_call(
        kernel,
        out_shape=jax.ShapeDtypeStruct((2 * frames, 4, 16, 256), F32),
        in_specs=[scalars, scalars] + [anywhere] * 7,
        out_specs=anywhere,
        scratch_shapes=[buffer(*array.shape) for array in arrays]
        + [buffer(3, frames, 16, 512)]
        + [buffer(frames, 32, 512)] * 4
        + [buffer(frames, 16, 512), buffer(frames, 32, 512)]
        + [buffer(*shape, kind=jnp.int32) for shape in ((8, 128), (5, 8, 128), (3, 8, 128))]
        + [buffer(8, 128), buffer(16, 8, 128)] * 2
        + [buffer(2, *time_weight.shape, kind=BF16), buffer(2, 9, 512, 256, kind=BF16)]
        + [buffer(2, frames + 2, 32, 512, kind=BF16), buffer(most * 32, 1024), buffer(9, 2, most * 32, 512, kind=BF16)]
        + [buffer(2, most * 2, 4, 16, 128), buffer(2 * frames, 4, 16, 256)]
        + sems(3, frames) + sems(frames) * 2 + sems(5, frames) + sems(5) + sems(16) * 2
        + [pltpu.SemaphoreType.DMA((len(arrays),)), pltpu.SemaphoreType.DMA((frames,))],
        compiler_params=pltpu.CompilerParams(
            collective_id=0, has_side_effects=True, vmem_limit_bytes=58 * 2**20
        ),
    )(offsets, lengths, *arrays)


def on_device(features, lengths, offsets, norm_gain, norm_bias, time_weight, time_bias, space_weight, space_bias):
    frames, channels = features.shape[2], features.shape[-1]
    row = lambda array: array.reshape(1, -1)
    result = decoded(
        offsets, lengths, features.reshape(frames, 16, channels), row(norm_gain), row(norm_bias),
        time_weight, row(time_bias), space_weight, row(space_bias),
    )
    return result[None, None]


def solution(mesh):
    in_specs = (P("grp", "tile", None, None, None, None), P(), P("tile"), P(), P(), P(), P(), P(), P())
    out_specs = P("grp", "tile", None, None, None, None)
    return jax.shard_map(on_device, mesh=mesh, in_specs=in_specs, out_specs=out_specs, check_vma=False)
```

time: 73.7 us -> 49.3 us (0.67)
  the two profiles are of different devices: /device:TPU:8 before, /device:TPU:1 now
where the time goes in v1:
time: 49.3 us; the launch traced here: 49.1 us
  Pallas kernels  46.1 us (94%)
  local copies, waits for them, and re-layouts  2.41 us (5%)
  between operations  0.66 us (1%)
    pallas_call x1, Pallas kernels, decoded(): pl.pallas_call(kernel, out_shape=jax.ShapeDtypeStruct((2 * frames, 4, 16,...  46.1 us
    unnamed x1, local copies, waits for them, and re-layouts  2.41 us

profile of v1, /device:TPU:1, one launch (start us, length us, event | category | flops | bytes accessed | tf_op | source)
XLA Modules:
  0.0 49.1 jit_solution(12460575182276867867)
XLA Ops:
  0.7 46.1 %shard_map.91 = f32[18,4,16,256]{3,2,1,0:T(8,128)} custom-call(s32[1]{0:T(128)S(6)} %copy.11.offsets, s32[16]{0:T(128)} %lengths.1, f32[9,16,512]{2,1,0:T(8,128)} %bitcast.7, f32[1,512]{1,0:T(1,128)} %bitcast.9, f32[1,512]{1,0:T(1,128)} %bitcast.10, f32[3,512,1024]{2,1,0:T(8,128)} %time_in.1, f32[1,1024]{1,0:T(1,128)} %bitcast.8, ...), custom_call_target="tpu_custom_call" | custom-call | tf_op jit(solution)/shard_map/pallas_call | solution.py:405
  46.7 2.4 %copy.12 = f32[1,1,18,4,16,256]{5,4,3,2,1,0:T(8,128)} copy(f32[1,1,18,4,16,256]{5,4,3,2,1,0:T(8,128)} %bitcast.6) | data formatting | bytes 2359296

commit v2 on v1

--- a/solution.py
+++ b/solution.py
@@ -130,9 +130,9 @@
     return other + column, own + right, own + left, other + right, other + left
 
 
-CORE_AFTER, HALO_AFTER = 2, 3
-CHUNKS = (3, 3, 3)
-LOOPED = 8
+CORE_AFTER, HALO_AFTER = 3, 4
+CHUNKS = (4, 3, 2)
+LOOPED = 9
 
 
 def kernel(
@@ -192,7 +192,6 @@
     def norms_copy(step):
         return send(norms, norms_in.at[step], norms_sem, step, (grp ^ step, tile))
 
-    block[:, 24:32] = jnp.zeros((frames, 8, 512), F32)
     barrier = pltpu.get_barrier_semaphore()
 
     @pl.loop(1, 16)
@@ -201,8 +200,16 @@
         pl.semaphore_signal(barrier, inc=1, device_id=(grp ^ step, tile), device_id_type=MESH)
 
     marks[...] = jnp.full(marks.shape, offsets[0], jnp.int32)
-    swap_out[:, 24:32] = jnp.zeros((frames, 8, 512), F32)
     act[:, 0:2] = jnp.zeros((2, 2, 32, 512), BF16)
+    pl.semaphore_wait(barrier, 30)
+    for kind in range(5):
+        mark_copy(kind).start()
+
+    @pl.loop(0, frames)
+    def _(frame):
+        for step in (1, 2, 3):
+            near_copy(step, frame).start()
+
     length = lengths[grp]
     loads[0].wait()
     total, squares = jnp.zeros((8, 512), F32), jnp.zeros((8, 512), F32)
@@ -215,18 +222,9 @@
         sums[part : part + 1] = total[:, part * 128 : part * 128 + 128]
         sums[part + 4 : part + 5] = squares[:, part * 128 : part * 128 + 128]
 
-    pl.semaphore_wait(barrier, 30)
-    for kind in range(5):
-        mark_copy(kind).start()
-
     @pl.loop(1, 16)
     def _(step):
         sums_copy(step).start()
-
-    @pl.loop(0, frames)
-    def _(frame):
-        for step in (1, 2, 3):
-            near_copy(step, frame).start()
 
     for kind in range(5):
         mark_copy(kind).wait_recv()

time: 49.3 us -> 51.3 us (1.041)
  Pallas kernels: 46.1 us -> 47.6 us
    pallas_call x1, Pallas kernels: 46.1 us -> 47.6 us  [decoded(): pl.pallas_call(kernel, out_shape=jax.ShapeDtypeStruct((2 * frames, 4, 16,...]
where the time goes in v2:
time: 51.3 us; the launch traced here: 50.7 us
  Pallas kernels  47.6 us (93%)
  local copies, waits for them, and re-layouts  2.41 us (5%)
  between operations  0.66 us (1%)
    pallas_call x1, Pallas kernels, decoded(): pl.pallas_call(kernel, out_shape=jax.ShapeDtypeStruct((2 * frames, 4, 16,...  47.6 us
    unnamed x1, local copies, waits for them, and re-layouts  2.41 us

profile of v2, /device:TPU:1, one launch (start us, length us, event | category | flops | bytes accessed | tf_op | source)
XLA Modules:
  0.0 50.7 jit_solution(13738348550300144906)
XLA Ops:
  0.7 47.6 %shard_map.91 = f32[18,4,16,256]{3,2,1,0:T(8,128)} custom-call(s32[1]{0:T(128)S(6)} %copy.11.offsets, s32[16]{0:T(128)} %lengths.1, f32[9,16,512]{2,1,0:T(8,128)} %bitcast.7, f32[1,512]{1,0:T(1,128)} %bitcast.9, f32[1,512]{1,0:T(1,128)} %bitcast.10, f32[3,512,1024]{2,1,0:T(8,128)} %time_in.1, f32[1,1024]{1,0:T(1,128)} %bitcast.8, ...), custom_call_target="tpu_custom_call" | custom-call | tf_op jit(solution)/shard_map/pallas_call | solution.py:403
  48.2 2.4 %copy.12 = f32[1,1,18,4,16,256]{5,4,3,2,1,0:T(8,128)} copy(f32[1,1,18,4,16,256]{5,4,3,2,1,0:T(8,128)} %bitcast.6) | data formatting | bytes 2359296

commit v3 on v2

--- a/solution.py
+++ b/solution.py
@@ -39,7 +39,7 @@
         act[0, frame + 2], act[1, frame + 2] = split(inner)
 
 
-def decode(first, frames, keep, upper, has_left, has_right, act, time, time_bias, space, space_bias, temporal, ops, stage, out):
+def decode(first, frames, keep, facing, upper, has_left, has_right, act, time, time_bias, space, space_bias, temporal, ops, stage, out):
     rows, depth = frames * 32, act.shape[-1]
     both, high = [], []
     for tap in range(3):
@@ -56,12 +56,15 @@
     for frame in range(frames):
         for half in range(2):
             lanes = slice(half * depth, half * depth + depth)
-            block = lambda i: temporal[frame * 32 + i * 8 : frame * 32 + i * 8 + 8, lanes]
-            row0, row1, across, side = block(0), block(1), block(2), block(3)
+            block = lambda i: temporal[pl.ds(pl.multiple_of(frame * 32 + i * 8, 8), 8), lanes]
+            side = lambda i: temporal[pl.ds(frame * 32 + 24 + i, 1), lanes]
+            other = 1 - facing
             columns = []
-            for row, left, right in ((row0, 0, 2), (row1, 1, 3), (across, 4, 5)):
-                before = jnp.where(place == 0, side[left : left + 1] * has_left, pltpu.roll(row, 1, 0))
-                after = jnp.where(place == 7, side[right : right + 1] * has_right, pltpu.roll(row, 7, 0))
+            for row, left, right in (
+                (block(facing), facing, 2 + facing), (block(other), other, 2 + other), (block(2), 4, 5),
+            ):
+                before = jnp.where(place == 0, side(left) * has_left, pltpu.roll(row, 1, 0))
+                after = jnp.where(place == 7, side(right) * has_right, pltpu.roll(row, 7, 0))
                 columns.append((before - row, row, after - row))
             start = (frame * 2 + half) * 16
             for b in range(3):
@@ -106,9 +109,10 @@
 MESH = pl.DeviceIdType.MESH
 ACROSS, RIGHT, LEFT, ACROSS_RIGHT, ACROSS_LEFT = range(5)
 MIRROR = (ACROSS, LEFT, RIGHT, ACROSS_LEFT, ACROSS_RIGHT)
-SIDES = (RIGHT, RIGHT, LEFT, LEFT, ACROSS_RIGHT, ACROSS_LEFT)
-PIECES = ((0, 8, 16), (8, 2, 24), (10, 2, 26), (12, 1, 28), (13, 1, 29))
-SENT = 32
+DIAGONALS, SIDES = (ACROSS_RIGHT, ACROSS_LEFT), (RIGHT, RIGHT, LEFT, LEFT)
+PIECES = ((0, 8, 16), (16, 2, 24), (18, 2, 26), (8, 1, 28), (9, 1, 29))
+VERTICAL, ENDS, FACING, SIDE, OTHER = range(5)
+PLACES = ((0, 8), (8, 2), (16, 8), (24, 4), (32, 8))
 
 
 def wide(value, times=4):
@@ -130,9 +134,10 @@
     return other + column, own + right, own + left, other + right, other + left
 
 
-CORE_AFTER, HALO_AFTER = 3, 4
-CHUNKS = (4, 3, 2)
-LOOPED = 9
+MARKS_AT, OWN_AFTER, CORE_AFTER, HALO_AFTER = 4, 2, 8, 10
+CHUNKS = (3, 3, 3)
+SIDE_AFTER, LEAD = 6, 6
+NORMS_AT = 6
 
 
 def kernel(
@@ -143,7 +148,7 @@
     time, space, act, temporal, ops, stage, out,
     near_sem, swap_sem, core_sem, halo_sem, mark_sem, sums_sem, norms_sem, load_sem, store_sem,
 ):
-    frames = features.shape[0]
+    frames = raw_features.shape[0]
     grp, tile = lax.axis_index("grp"), lax.axis_index("tile")
     neighbours = tile_neighbours(tile)
     facing = 1 - tile // 8
@@ -151,11 +156,12 @@
     loads = [
         pltpu.make_async_copy(source, target, load_sem.at[at])
         for at, (source, target) in enumerate((
-            (raw_features, features), (time_in, time_raw), (space_in, space_raw), (gain_in, gain),
+            (raw_features.at[:, pl.ds(pl.multiple_of(facing * 8, 8), 8)], features.at[0]), (time_in, time_raw), (space_in, space_raw), (gain_in, gain),
             (bias_in, bias), (time_bias_in, time_bias), (space_bias_in, space_bias),
+            (raw_features.at[:, pl.ds(pl.multiple_of(8 - facing * 8, 8), 8)], features.at[1]),
         ))
     ]
-    for load in loads:
+    for load in loads[7:] + loads[:7]:
         load.start()
 
     def send(source, target, sems, at, device):
@@ -165,16 +171,18 @@
             device_id=device, device_id_type=MESH,
         )
 
-    def near_copy(step, frame):
-        return send(raw_features.at[frame], near.at[step - 1, frame], near_sem, (step - 1, frame), (grp ^ (step * 2), tile))
-
-    def swap_copy(frame):
-        rows = pl.ds(0, SENT)
-        return send(swap_out.at[frame, rows], swap_in.at[frame, rows], swap_sem, frame, (grp ^ 8, tile))
-
-    def core_copy(frame):
-        rows = pl.ds(0, SENT)
-        return send(core_out.at[frame, rows], core_in.at[frame, rows], core_sem, frame, (grp ^ 1, tile))
+    def near_copy(step, half, frame):
+        start = facing * 8 if half == 0 else 8 - facing * 8
+        source = raw_features.at[frame, pl.ds(pl.multiple_of(start, 8), 8)]
+        return send(source, near.at[step - 1, half, frame], near_sem, (step - 1, half, frame), (grp ^ (step * 2), tile))
+
+    def swap_copy(part, frame):
+        rows = pl.ds(*PLACES[part])
+        return send(swap_out.at[frame, rows], swap_in.at[frame, rows], swap_sem, (part, frame), (grp ^ 8, tile))
+
+    def core_copy(part, frame):
+        rows = pl.ds(*PLACES[part])
+        return send(core_out.at[frame, rows], core_in.at[frame, rows], core_sem, (part, frame), (grp ^ 1, tile))
 
     def halo_copy(kind, frame):
         start, count, land = PIECES[kind]
@@ -205,17 +213,18 @@
     for kind in range(5):
         mark_copy(kind).start()
 
-    @pl.loop(0, frames)
+    @pl.loop(0, LEAD)
     def _(frame):
         for step in (1, 2, 3):
-            near_copy(step, frame).start()
+            near_copy(step, 0, frame).start()
 
     length = lengths[grp]
     loads[0].wait()
+    loads[7].wait()
     total, squares = jnp.zeros((8, 512), F32), jnp.zeros((8, 512), F32)
     for frame in range(frames):
         for row in range(2):
-            value = jnp.where(frame < length, features[frame, row * 8 : row * 8 + 8], 0.0)
+            value = jnp.where(frame < length, features[row, frame], 0.0)
             total, squares = total + value, squares + value * value
     total, squares = jnp.sum(total, axis=0, keepdims=True), jnp.sum(squares, axis=0, keepdims=True)
     for part in range(4):
@@ -226,50 +235,69 @@
     def _(step):
         sums_copy(step).start()
 
-    for kind in range(5):
-        mark_copy(kind).wait_recv()
     kinds[0] = marks[...]
-    kinds[1] = mark_in[ACROSS]
-    kinds[2] = jnp.concatenate([mark_in[kind][0:1] for kind in SIDES] + [marks[0:2]], axis=0)
-
-    def chosen(rows, frame, mark):
+
+    def chosen(half, rows, frame, mark):
         pick = wide(mark // 2 % 4)
-        value = features[frame, rows]
+        value = features[half, frame, rows]
         for step in (1, 2, 3):
-            value = jnp.where(pick == step, near[step - 1, frame, rows], value)
+            value = jnp.where(pick == step, near[step - 1, half, frame, rows], value)
         return value
 
-    def start_swap(frame):
+    def learn_marks():
+        for kind in range(5):
+            mark_copy(kind).wait_recv()
+        kinds[1] = mark_in[ACROSS]
+        for at, picked in ((2, DIAGONALS), (3, SIDES)):
+            kinds[at] = jnp.concatenate([mark_in[kind][0:1] for kind in picked] + [marks[len(picked) :]], axis=0)
+
+    def wait_near(half, frame):
         for step in (1, 2, 3):
-            near_copy(step, frame).wait_recv()
-        for row in range(2):
-            swap_out[frame, row * 8 : row * 8 + 8] = chosen(pl.ds(row * 8, 8), frame, kinds[0])
-        swap_out[frame, 16:24] = chosen(pl.ds(pl.multiple_of(facing * 8, 8), 8), frame, kinds[1])
-        for place, source in enumerate((7, 15, 0, 8, facing * 8 + 7, facing * 8)):
-            mark = kinds[2, place : place + 1]
-            swap_out[frame, 24 + place : 25 + place] = chosen(pl.ds(source, 1), frame, mark)
-        swap_copy(frame).start()
-
-    def start_core(frame):
-        swap_copy(frame).wait_recv()
-        for part, kind in enumerate((0, 0, 1, 2)):
-            rows = slice(part * 8, part * 8 + 8)
-            crossed = wide(kinds[kind]) // 8 == 1
-            core_out[frame, rows] = jnp.where(crossed, swap_in[frame, rows], swap_out[frame, rows])
-        core_copy(frame).start()
-
-    def start_halo(frame):
-        core_copy(frame).wait_recv()
-        for part, kind in enumerate((0, 0, 1, 2)):
-            rows = slice(part * 8, part * 8 + 8)
-            crossed = wide(kinds[kind]) % 2 == 1
-            value = jnp.where(crossed, core_in[frame, rows], core_out[frame, rows])
-            if part < 2:
-                block[frame, rows] = value
-            else:
-                halo[frame, part * 8 - 16 : part * 8 - 8] = value
-        for kind in range(5):
+            near_copy(step, half, frame).wait_recv()
+
+    def swap_part(part, frame):
+        start, count = PLACES[part]
+        rows = pl.ds(0, 8)
+        if part == VERTICAL:
+            swap_out[frame, start : start + 8] = chosen(0, rows, frame, kinds[1])
+        elif part in (FACING, OTHER):
+            swap_out[frame, start : start + 8] = chosen(int(part == OTHER), rows, frame, kinds[0])
+        else:
+            cells = ((0, 7), (0, 0)) if part == ENDS else ((0, 7), (1, 7), (0, 0), (1, 0))
+            for place, (half, cell) in enumerate(cells):
+                mark = kinds[2 if part == ENDS else 3, place : place + 1]
+                swap_out[frame, start + place : start + place + 1] = chosen(half, pl.ds(cell, 1), frame, mark)
+        swap_copy(part, frame).start()
+
+    def mark_of(part):
+        return wide(kinds[(1, 2, 0, 3, 0)[part]])
+
+    def core_part(part, frame):
+        swap_copy(part, frame).wait_recv()
+        rows = slice(PLACES[part][0], PLACES[part][0] + 8)
+        crossed = mark_of(part) // 8 == 1
+        core_out[frame, rows] = jnp.where(crossed, swap_in[frame, rows], swap_out[frame, rows])
+        core_copy(part, frame).start()
+
+    def final(part, frame):
+        core_copy(part, frame).wait_recv()
+        rows = slice(PLACES[part][0], PLACES[part][0] + 8)
+        return jnp.where(mark_of(part) % 2 == 1, core_in[frame, rows], core_out[frame, rows])
+
+    def send_vertical(frame):
+        for part, kinds_sent in ((VERTICAL, (ACROSS,)), (ENDS, DIAGONALS)):
+            halo[frame, part * 8 : part * 8 + 8] = final(part, frame)
+            for kind in kinds_sent:
+                halo_copy(kind, frame).start()
+
+    def send_sides(frame):
+        halo[frame, 16:24] = final(SIDE, frame)
+        for kind in (RIGHT, LEFT):
             halo_copy(kind, frame).start()
+
+    def finish(frame):
+        block[frame, 0:8] = final(FACING, frame)
+        block[frame, 8:16] = final(OTHER, frame)
 
     def start_norms():
         @pl.loop(1, 16)
@@ -288,42 +316,100 @@
         def _(other):
             norms_copy(other).start()
 
-    @pl.loop(0, LOOPED)
+    def swap_vertical(frame):
+        swap_part(VERTICAL, frame)
+        swap_part(ENDS, frame)
+
+    def core_vertical(frame):
+        core_part(VERTICAL, frame)
+        core_part(ENDS, frame)
+
+    def start_near(step):
+        for half in range(2):
+            @pl.when((step >= half * frames) & (step < half * frames + frames))
+            def _():
+                for other in (1, 2, 3):
+                    near_copy(other, half, step - half * frames).start()
+
+    @pl.loop(0, frames)
     def _(step):
-        start_swap(step)
+        start_near(step + LEAD)
+        wait_near(0, step)
+
+        @pl.when(step < MARKS_AT)
+        def _():
+            swap_part(FACING, step)
+
+        @pl.when(step == MARKS_AT)
+        def _():
+            learn_marks()
+            for frame in range(MARKS_AT):
+                swap_vertical(frame)
+
+        @pl.when(step >= MARKS_AT)
+        def _():
+            swap_vertical(step)
+
+        @pl.when(step >= MARKS_AT + OWN_AFTER)
+        def _():
+            swap_part(FACING, step - OWN_AFTER)
 
         @pl.when(step >= CORE_AFTER)
         def _():
-            start_core(step - CORE_AFTER)
-
-        @pl.when(step >= HALO_AFTER)
-        def _():
-            start_halo(step - HALO_AFTER)
+            core_vertical(step - CORE_AFTER)
 
         @pl.when(step == 0)
         def _():
             loads[1].wait()
             loads[2].wait()
 
-        @pl.when(step < 4)
-        def _():
-            @pl.loop(0, 6)
-            def _(piece):
-                prepare_time(step * 6 + piece, time_raw, time)
-
-            @pl.loop(0, 4)
-            def _(piece):
-                prepare_space(step * 4 + piece, space_raw, space)
-
-        @pl.when(step == 1)
+        @pl.when(step < 8)
+        def _():
+            for piece in range(3):
+                prepare_time(step * 3 + piece, time_raw, time)
+            for piece in range(2):
+                prepare_space(step * 2 + piece, space_raw, space)
+
+        @pl.when(step == NORMS_AT)
         def _():
             start_norms()
+
+    @pl.loop(0, frames)
+    def _(frame):
+        step = frame + frames
+        start_near(step + LEAD)
+        wait_near(1, frame)
+        swap_part(SIDE, frame)
+        swap_part(OTHER, frame)
+
+        @pl.when(frame < OWN_AFTER)
+        def _():
+            swap_part(FACING, step - OWN_AFTER)
+
+        @pl.when(step < frames + CORE_AFTER)
+        def _():
+            core_vertical(step - CORE_AFTER)
+
+        @pl.when(step >= HALO_AFTER)
+        def _():
+            send_vertical(step - HALO_AFTER)
+
+        core_part(FACING, frame)
+
+        @pl.when(frame >= SIDE_AFTER)
+        def _():
+            core_part(SIDE, frame - SIDE_AFTER)
+            core_part(OTHER, frame - SIDE_AFTER)
+
+        @pl.when(frame >= SIDE_AFTER + 1)
+        def _():
+            send_sides(frame - SIDE_AFTER - 1)
 
     @pl.loop(1, 16)
     def _(other):
         norms_copy(other).wait_recv()
 
-    for load in loads[3:]:
+    for load in loads[3:7]:
         load.wait()
     value = norms[...]
     for other in range(1, 16):
@@ -348,26 +434,36 @@
             normalize(first, count, block, mean, scale, gain[...], bias[...], act)
             yield
             yield from decode(
-                first, count, keep, upper, has_left, has_right, act, time, time_bias, space, space_bias,
+                first, count, keep, facing, upper, has_left, has_right, act, time, time_bias, space, space_bias,
                 temporal, ops, stage, out,
             )
             store(first, count).start()
             first += count
 
     def transfers():
-        for step in range(LOOPED, frames + HALO_AFTER):
-            if step < frames:
-                start_swap(step)
-                yield
-            if step < frames + CORE_AFTER:
-                start_core(step - CORE_AFTER)
-                yield
-            start_halo(step - HALO_AFTER)
+        left = frames - SIDE_AFTER
+        for frame in range(2 * frames - HALO_AFTER, frames):
+            send_vertical(frame)
+        for frame in range(left, left + 2):
+            core_part(SIDE, frame)
+            core_part(OTHER, frame)
+            send_sides(frame - 1)
+        for frame in range(left):
+            finish(frame)
+        yield
+        for frame in range(left + 2, frames):
+            core_part(SIDE, frame)
+            core_part(OTHER, frame)
+            send_sides(frame - 1)
+            finish(frame - 2)
             yield
+        send_sides(frames - 1)
+        for frame in range(frames - 2, frames):
+            finish(frame)
 
     work, moves = compute(), transfers()
     for _ in moves:
-        next(work, None)
+        next(work)
     for _ in work:
         pass
 
@@ -385,10 +481,12 @@
 
     @pl.loop(0, frames)
     def _(frame):
-        for step in (1, 2, 3):
-            near_copy(step, frame).wait_send()
-        swap_copy(frame).wait_send()
-        core_copy(frame).wait_send()
+        for half in range(2):
+            for step in (1, 2, 3):
+                near_copy(step, half, frame).wait_send()
+        for part in range(5):
+            swap_copy(part, frame).wait_send()
+            core_copy(part, frame).wait_send()
         for kind in range(5):
             halo_copy(kind, frame).wait_send()
 
@@ -405,17 +503,17 @@
         out_shape=jax.ShapeDtypeStruct((2 * frames, 4, 16, 256), F32),
         in_specs=[scalars, scalars] + [anywhere] * 7,
         out_specs=anywhere,
-        scratch_shapes=[buffer(*array.shape) for array in arrays]
-        + [buffer(3, frames, 16, 512)]
-        + [buffer(frames, 32, 512)] * 4
-        + [buffer(frames, 16, 512), buffer(frames, 32, 512)]
-        + [buffer(*shape, kind=jnp.int32) for shape in ((8, 128), (5, 8, 128), (3, 8, 128))]
+        scratch_shapes=[buffer(2, frames, 8, 512)] + [buffer(*array.shape) for array in arrays[1:]]
+        + [buffer(3, 2, frames, 8, 512)]
+        + [buffer(frames, 40, 512)] * 4
+        + [buffer(frames, 24, 512), buffer(frames, 32, 512)]
+        + [buffer(*shape, kind=jnp.int32) for shape in ((8, 128), (5, 8, 128), (4, 8, 128))]
         + [buffer(8, 128), buffer(16, 8, 128)] * 2
         + [buffer(2, *time_weight.shape, kind=BF16), buffer(2, 9, 512, 256, kind=BF16)]
         + [buffer(2, frames + 2, 32, 512, kind=BF16), buffer(most * 32, 1024), buffer(9, 2, most * 32, 512, kind=BF16)]
         + [buffer(2, most * 2, 4, 16, 128), buffer(2 * frames, 4, 16, 256)]
-        + sems(3, frames) + sems(frames) * 2 + sems(5, frames) + sems(5) + sems(16) * 2
-        + [pltpu.SemaphoreType.DMA((len(arrays),)), pltpu.SemaphoreType.DMA((frames,))],
+        + sems(3, 2, frames) + sems(5, frames) * 3 + sems(5) + sems(16) * 2
+        + [pltpu.SemaphoreType.DMA((len(arrays) + 1,)), pltpu.SemaphoreType.DMA((frames,))],
         compiler_params=pltpu.CompilerParams(
             collective_id=0, has_side_effects=True, vmem_limit_bytes=58 * 2**20
         ),

time: 51.3 us -> 52.9 us (1.031); the launches traced: 50.7 us -> 52.8 us
  Pallas kernels: 47.6 us -> 49.7 us
    pallas_call x1, Pallas kernels: 47.6 us -> 49.7 us  [decoded(): pl.pallas_call(kernel, out_shape=jax.ShapeDtypeStruct((2 * frames, 4, 16,...]
where the time goes in v3:
time: 52.9 us; the launch traced here: 52.8 us
  Pallas kernels  49.7 us (94%)
  local copies, waits for them, and re-layouts  2.41 us (5%)
  between operations  0.66 us (1%)
    pallas_call x1, Pallas kernels, decoded(): pl.pallas_call(kernel, out_shape=jax.ShapeDtypeStruct((2 * frames, 4, 16,...  49.7 us
    unnamed x1, local copies, waits for them, and re-layouts  2.41 us

profile of v3, /device:TPU:1, one launch (start us, length us, event | category | flops | bytes accessed | tf_op | source)
XLA Modules:
  0.0 52.8 jit_solution(5350377376878342790)
XLA Ops:
  0.7 49.7 %shard_map.91 = f32[18,4,16,256]{3,2,1,0:T(8,128)} custom-call(s32[1]{0:T(128)S(6)} %copy.11.offsets, s32[16]{0:T(128)} %lengths.1, f32[9,16,512]{2,1,0:T(8,128)} %bitcast.7, f32[1,512]{1,0:T(1,128)} %bitcast.9, f32[1,512]{1,0:T(1,128)} %bitcast.10, f32[3,512,1024]{2,1,0:T(8,128)} %time_in.1, f32[1,1024]{1,0:T(1,128)} %bitcast.8, ...), custom_call_target="tpu_custom_call" | custom-call | tf_op jit(solution)/shard_map/pallas_call | solution.py:501
  50.4 2.4 %copy.12 = f32[1,1,18,4,16,256]{5,4,3,2,1,0:T(8,128)} copy(f32[1,1,18,4,16,256]{5,4,3,2,1,0:T(8,128)} %bitcast.6) | data formatting | bytes 2359296

commit v4 on v3

--- a/solution.py
+++ b/solution.py
@@ -63,8 +63,8 @@
             for row, left, right in (
                 (block(facing), facing, 2 + facing), (block(other), other, 2 + other), (block(2), 4, 5),
             ):
-                before = jnp.where(place == 0, side(left) * has_left, pltpu.roll(row, 1, 0))
-                after = jnp.where(place == 7, side(right) * has_right, pltpu.roll(row, 7, 0))
+                before = jnp.where(place == 0, jnp.where(has_left, side(left), 0.0), pltpu.roll(row, 1, 0))
+                after = jnp.where(place == 7, jnp.where(has_right, side(right), 0.0), pltpu.roll(row, 7, 0))
                 columns.append((before - row, row, after - row))
             start = (frame * 2 + half) * 16
             for b in range(3):
@@ -134,10 +134,7 @@
     return other + column, own + right, own + left, other + right, other + left
 
 
-MARKS_AT, OWN_AFTER, CORE_AFTER, HALO_AFTER = 4, 2, 8, 10
-CHUNKS = (3, 3, 3)
-SIDE_AFTER, LEAD = 6, 6
-NORMS_AT = 6
+GROUP = 3
 
 
 def kernel(
@@ -149,9 +146,11 @@
     near_sem, swap_sem, core_sem, halo_sem, mark_sem, sums_sem, norms_sem, load_sem, store_sem,
 ):
     frames = raw_features.shape[0]
+    groups = frames // GROUP
     grp, tile = lax.axis_index("grp"), lax.axis_index("tile")
     neighbours = tile_neighbours(tile)
     facing = 1 - tile // 8
+    has_left, has_right = tile % 8 != 0, tile % 8 != 7
 
     loads = [
         pltpu.make_async_copy(source, target, load_sem.at[at])
@@ -171,25 +170,43 @@
             device_id=device, device_id_type=MESH,
         )
 
-    def near_copy(step, half, frame):
+    def near_copy(step, half, group):
         start = facing * 8 if half == 0 else 8 - facing * 8
-        source = raw_features.at[frame, pl.ds(pl.multiple_of(start, 8), 8)]
-        return send(source, near.at[step - 1, half, frame], near_sem, (step - 1, half, frame), (grp ^ (step * 2), tile))
-
-    def swap_copy(part, frame):
+        source = raw_features.at[pl.ds(group * GROUP, GROUP), pl.ds(pl.multiple_of(start, 8), 8)]
+        return send(source, near.at[step - 1, half, pl.ds(group * GROUP, GROUP)], near_sem, (step - 1, half, group), (grp ^ (step * 2), tile))
+
+    def swap_copy(part, group):
         rows = pl.ds(*PLACES[part])
-        return send(swap_out.at[frame, rows], swap_in.at[frame, rows], swap_sem, (part, frame), (grp ^ 8, tile))
-
-    def core_copy(part, frame):
+        at = pl.ds(group * GROUP, GROUP)
+        return send(swap_out.at[at, rows], swap_in.at[at, rows], swap_sem, (part, group), (grp ^ 8, tile))
+
+    def core_copy(part, group):
         rows = pl.ds(*PLACES[part])
-        return send(core_out.at[frame, rows], core_in.at[frame, rows], core_sem, (part, frame), (grp ^ 1, tile))
-
-    def halo_copy(kind, frame):
+        at = pl.ds(group * GROUP, GROUP)
+        return send(core_out.at[at, rows], core_in.at[at, rows], core_sem, (part, group), (grp ^ 1, tile))
+
+    def halo_copy(kind, group):
         start, count, land = PIECES[kind]
+        at = pl.ds(group * GROUP, GROUP)
         return send(
-            halo.at[frame, pl.ds(start, count)], block.at[frame, pl.ds(land, count)],
-            halo_sem, (kind, frame), (grp, neighbours[kind]),
+            halo.at[at, pl.ds(start, count)], block.at[at, pl.ds(land, count)],
+            halo_sem, (kind, group), (grp, neighbours[kind]),
         )
+
+    def where_there(kind, there_right, there_left, action):
+        if kind == ACROSS:
+            action()
+        else:
+            pl.when(there_right if kind in (RIGHT, ACROSS_RIGHT) else there_left)(action)
+
+    def start_piece(kind, group):
+        where_there(kind, has_right, has_left, lambda: halo_copy(kind, group).start())
+
+    def piece_sent(kind, group):
+        where_there(kind, has_right, has_left, lambda: halo_copy(kind, group).wait_send())
+
+    def piece_landed(kind, group):
+        where_there(kind, has_left, has_right, lambda: halo_copy(kind, group).wait_recv())
 
     def mark_copy(kind):
         return send(marks, mark_in.at[MIRROR[kind]], mark_sem, MIRROR[kind], (grp, neighbours[kind]))
@@ -213,10 +230,12 @@
     for kind in range(5):
         mark_copy(kind).start()
 
-    @pl.loop(0, LEAD)
-    def _(frame):
-        for step in (1, 2, 3):
-            near_copy(step, 0, frame).start()
+    def start_near(half):
+        for group in range(groups):
+            for step in (1, 2, 3):
+                near_copy(step, half, group).start()
+
+    start_near(0)
 
     length = lengths[grp]
     loads[0].wait()
@@ -235,6 +254,8 @@
     def _(step):
         sums_copy(step).start()
 
+    start_near(1)
+
     kinds[0] = marks[...]
 
     def chosen(half, rows, frame, mark):
@@ -251,53 +272,60 @@
         for at, picked in ((2, DIAGONALS), (3, SIDES)):
             kinds[at] = jnp.concatenate([mark_in[kind][0:1] for kind in picked] + [marks[len(picked) :]], axis=0)
 
-    def wait_near(half, frame):
+    def wait_near(half, group):
         for step in (1, 2, 3):
-            near_copy(step, half, frame).wait_recv()
-
-    def swap_part(part, frame):
+            near_copy(step, half, group).wait_recv()
+
+    def members(group):
+        return range(group * GROUP, group * GROUP + GROUP)
+
+    def swap_part(part, group):
         start, count = PLACES[part]
         rows = pl.ds(0, 8)
-        if part == VERTICAL:
-            swap_out[frame, start : start + 8] = chosen(0, rows, frame, kinds[1])
-        elif part in (FACING, OTHER):
-            swap_out[frame, start : start + 8] = chosen(int(part == OTHER), rows, frame, kinds[0])
-        else:
-            cells = ((0, 7), (0, 0)) if part == ENDS else ((0, 7), (1, 7), (0, 0), (1, 0))
-            for place, (half, cell) in enumerate(cells):
-                mark = kinds[2 if part == ENDS else 3, place : place + 1]
-                swap_out[frame, start + place : start + place + 1] = chosen(half, pl.ds(cell, 1), frame, mark)
-        swap_copy(part, frame).start()
+        for frame in members(group):
+            if part == VERTICAL:
+                swap_out[frame, start : start + 8] = chosen(0, rows, frame, kinds[1])
+            elif part in (FACING, OTHER):
+                swap_out[frame, start : start + 8] = chosen(int(part == OTHER), rows, frame, kinds[0])
+            else:
+                cells = ((0, 7), (0, 0)) if part == ENDS else ((0, 7), (1, 7), (0, 0), (1, 0))
+                for place, (half, cell) in enumerate(cells):
+                    mark = kinds[2 if part == ENDS else 3, place : place + 1]
+                    swap_out[frame, start + place : start + place + 1] = chosen(half, pl.ds(cell, 1), frame, mark)
+        swap_copy(part, group).start()
 
     def mark_of(part):
         return wide(kinds[(1, 2, 0, 3, 0)[part]])
 
-    def core_part(part, frame):
-        swap_copy(part, frame).wait_recv()
+    def core_part(part, group):
+        swap_copy(part, group).wait_recv()
         rows = slice(PLACES[part][0], PLACES[part][0] + 8)
         crossed = mark_of(part) // 8 == 1
-        core_out[frame, rows] = jnp.where(crossed, swap_in[frame, rows], swap_out[frame, rows])
-        core_copy(part, frame).start()
-
-    def final(part, frame):
-        core_copy(part, frame).wait_recv()
+        for frame in members(group):
+            core_out[frame, rows] = jnp.where(crossed, swap_in[frame, rows], swap_out[frame, rows])
+        core_copy(part, group).start()
+
+    def finals(part, group, target, at):
+        core_copy(part, group).wait_recv()
         rows = slice(PLACES[part][0], PLACES[part][0] + 8)
-        return jnp.where(mark_of(part) % 2 == 1, core_in[frame, rows], core_out[frame, rows])
-
-    def send_vertical(frame):
+        crossed = mark_of(part) % 2 == 1
+        for frame in members(group):
+            target[frame, at : at + 8] = jnp.where(crossed, core_in[frame, rows], core_out[frame, rows])
+
+    def send_vertical(group):
         for part, kinds_sent in ((VERTICAL, (ACROSS,)), (ENDS, DIAGONALS)):
-            halo[frame, part * 8 : part * 8 + 8] = final(part, frame)
+            finals(part, group, halo, part * 8)
             for kind in kinds_sent:
-                halo_copy(kind, frame).start()
-
-    def send_sides(frame):
-        halo[frame, 16:24] = final(SIDE, frame)
+                start_piece(kind, group)
+
+    def send_sides(group):
+        finals(SIDE, group, halo, 16)
         for kind in (RIGHT, LEFT):
-            halo_copy(kind, frame).start()
-
-    def finish(frame):
-        block[frame, 0:8] = final(FACING, frame)
-        block[frame, 8:16] = final(OTHER, frame)
+            start_piece(kind, group)
+
+    def finish(group):
+        finals(FACING, group, block, 0)
+        finals(OTHER, group, block, 8)
 
     def start_norms():
         @pl.loop(1, 16)
@@ -316,94 +344,63 @@
         def _(other):
             norms_copy(other).start()
 
-    def swap_vertical(frame):
-        swap_part(VERTICAL, frame)
-        swap_part(ENDS, frame)
-
-    def core_vertical(frame):
-        core_part(VERTICAL, frame)
-        core_part(ENDS, frame)
-
-    def start_near(step):
-        for half in range(2):
-            @pl.when((step >= half * frames) & (step < half * frames + frames))
-            def _():
-                for other in (1, 2, 3):
-                    near_copy(other, half, step - half * frames).start()
-
-    @pl.loop(0, frames)
-    def _(step):
-        start_near(step + LEAD)
-        wait_near(0, step)
-
-        @pl.when(step < MARKS_AT)
-        def _():
-            swap_part(FACING, step)
-
-        @pl.when(step == MARKS_AT)
-        def _():
-            learn_marks()
-            for frame in range(MARKS_AT):
-                swap_vertical(frame)
-
-        @pl.when(step >= MARKS_AT)
-        def _():
-            swap_vertical(step)
-
-        @pl.when(step >= MARKS_AT + OWN_AFTER)
-        def _():
-            swap_part(FACING, step - OWN_AFTER)
-
-        @pl.when(step >= CORE_AFTER)
-        def _():
-            core_vertical(step - CORE_AFTER)
-
-        @pl.when(step == 0)
-        def _():
-            loads[1].wait()
-            loads[2].wait()
-
-        @pl.when(step < 8)
-        def _():
-            for piece in range(3):
-                prepare_time(step * 3 + piece, time_raw, time)
-            for piece in range(2):
-                prepare_space(step * 2 + piece, space_raw, space)
-
-        @pl.when(step == NORMS_AT)
-        def _():
-            start_norms()
-
-    @pl.loop(0, frames)
-    def _(frame):
-        step = frame + frames
-        start_near(step + LEAD)
-        wait_near(1, frame)
-        swap_part(SIDE, frame)
-        swap_part(OTHER, frame)
-
-        @pl.when(frame < OWN_AFTER)
-        def _():
-            swap_part(FACING, step - OWN_AFTER)
-
-        @pl.when(step < frames + CORE_AFTER)
-        def _():
-            core_vertical(step - CORE_AFTER)
-
-        @pl.when(step >= HALO_AFTER)
-        def _():
-            send_vertical(step - HALO_AFTER)
-
-        core_part(FACING, frame)
-
-        @pl.when(frame >= SIDE_AFTER)
-        def _():
-            core_part(SIDE, frame - SIDE_AFTER)
-            core_part(OTHER, frame - SIDE_AFTER)
-
-        @pl.when(frame >= SIDE_AFTER + 1)
-        def _():
-            send_sides(frame - SIDE_AFTER - 1)
+    def swap_vertical(group):
+        swap_part(VERTICAL, group)
+        swap_part(ENDS, group)
+
+    def core_vertical(group):
+        core_part(VERTICAL, group)
+        core_part(ENDS, group)
+
+    def swap_other(group):
+        swap_part(SIDE, group)
+        swap_part(OTHER, group)
+
+    def core_other(group):
+        core_part(SIDE, group)
+        core_part(OTHER, group)
+
+    wait_near(0, 0)
+    swap_part(FACING, 0)
+    loads[1].wait()
+
+    @pl.loop(0, 24)
+    def _(piece):
+        prepare_time(piece, time_raw, time)
+
+    learn_marks()
+    swap_vertical(0)
+    wait_near(0, 1)
+    swap_vertical(1)
+    swap_part(FACING, 1)
+    loads[2].wait()
+
+    @pl.loop(0, 16)
+    def _(piece):
+        prepare_space(piece, space_raw, space)
+
+    wait_near(0, 2)
+    swap_vertical(2)
+    swap_part(FACING, 2)
+    start_norms()
+    core_vertical(0)
+    wait_near(1, 0)
+    swap_other(0)
+    core_vertical(1)
+    send_vertical(0)
+    core_part(FACING, 0)
+    wait_near(1, 1)
+    swap_other(1)
+    core_vertical(2)
+    send_vertical(1)
+    core_part(FACING, 1)
+    core_other(0)
+    wait_near(1, 2)
+    swap_other(2)
+    send_vertical(2)
+    send_sides(0)
+    core_part(FACING, 2)
+    finish(0)
 
     @pl.loop(1, 16)
     def _(other):
@@ -418,7 +415,7 @@
         jnp.concatenate([value[row + i : row + i + 1] for i in range(4)], axis=1) for row in (0, 4)
     )
     number = lambda flag: flag.astype(F32)
-    upper, has_left, has_right = number(tile < 8), number(tile % 8 != 0), number(tile % 8 != 7)
+    upper = number(tile < 8)
     keep = lengths[grp ^ offsets[0]]
 
     def store(first, count):
@@ -427,10 +424,9 @@
 
     def compute():
         first = 0
-        for count in CHUNKS:
-            for frame in range(first, first + count):
-                for kind in range(5):
-                    halo_copy(kind, frame).wait_recv()
+        for count in [GROUP] * groups:
+            for kind in range(5):
+                piece_landed(kind, first // GROUP)
             normalize(first, count, block, mean, scale, gain[...], bias[...], act)
             yield
             yield from decode(
@@ -441,25 +437,17 @@
             first += count
 
     def transfers():
-        left = frames - SIDE_AFTER
-        for frame in range(2 * frames - HALO_AFTER, frames):
-            send_vertical(frame)
-        for frame in range(left, left + 2):
-            core_part(SIDE, frame)
-            core_part(OTHER, frame)
-            send_sides(frame - 1)
-        for frame in range(left):
-            finish(frame)
+        core_other(1)
         yield
-        for frame in range(left + 2, frames):
-            core_part(SIDE, frame)
-            core_part(OTHER, frame)
-            send_sides(frame - 1)
-            finish(frame - 2)
-            yield
-        send_sides(frames - 1)
-        for frame in range(frames - 2, frames):
-            finish(frame)
+        send_sides(1)
+        yield
+        yield
+        core_other(2)
+        yield
+        finish(1)
+        yield
+        send_sides(2)
+        finish(2)
 
     work, moves = compute(), transfers()
     for _ in moves:
@@ -468,7 +456,7 @@
         pass
 
     first = 0
-    for count in CHUNKS:
+    for count in [GROUP] * groups:
         store(first, count).wait()
         first += count
     for kind in range(5):
@@ -479,16 +467,15 @@
         sums_copy(other).wait_send()
         norms_copy(other).wait_send()
 
-    @pl.loop(0, frames)
-    def _(frame):
+    for group in range(groups):
         for half in range(2):
             for step in (1, 2, 3):
-                near_copy(step, half, frame).wait_send()
+                near_copy(step, half, group).wait_send()
         for part in range(5):
-            swap_copy(part, frame).wait_send()
-            core_copy(part, frame).wait_send()
+            swap_copy(part, group).wait_send()
+            core_copy(part, group).wait_send()
         for kind in range(5):
-            halo_copy(kind, frame).wait_send()
+            piece_sent(kind, group)
 
 
 def decoded(offsets, lengths, features, gain, bias, time_weight, time_bias, space_weight, space_bias):
@@ -496,7 +483,7 @@
     scalars, anywhere = pl.BlockSpec(memory_space=pltpu.SMEM), pl.BlockSpec(memory_space=pl.ANY)
     sems = lambda *shape: [[pltpu.SemaphoreType.DMA(shape)] * 2]
     buffer = lambda *shape, kind=F32: pltpu.VMEM(shape, kind)
-    most = max(CHUNKS)
+    most = GROUP
     arrays = (features, gain, bias, time_weight, time_bias, space_weight, space_bias)
     return pl.pallas_call(
         kernel,
@@ -512,7 +499,7 @@
         + [buffer(2, *time_weight.shape, kind=BF16), buffer(2, 9, 512, 256, kind=BF16)]
         + [buffer(2, frames + 2, 32, 512, kind=BF16), buffer(most * 32, 1024), buffer(9, 2, most * 32, 512, kind=BF16)]
         + [buffer(2, most * 2, 4, 16, 128), buffer(2 * frames, 4, 16, 256)]
-        + sems(3, 2, frames) + sems(5, frames) * 3 + sems(5) + sems(16) * 2
+        + sems(3, 2, frames // GROUP) + sems(5, frames // GROUP) * 3 + sems(5) + sems(16) * 2
         + [pltpu.SemaphoreType.DMA((len(arrays) + 1,)), pltpu.SemaphoreType.DMA((frames,))],
         compiler_params=pltpu.CompilerParams(
             collective_id=0, has_side_effects=True, vmem_limit_bytes=58 * 2**20

time: 52.9 us -> 48.8 us (0.922)
  Pallas kernels: 49.7 us -> 45.2 us
    pallas_call x1, Pallas kernels: 49.7 us -> 45.2 us  [decoded(): pl.pallas_call(kernel, out_shape=jax.ShapeDtypeStruct((2 * frames, 4, 16,...]
where the time goes in v4:
time: 48.8 us; the launch traced here: 48.2 us
  Pallas kernels  45.2 us (93%)
  local copies, waits for them, and re-layouts  2.41 us (5%)
  between operations  0.66 us (1%)
    pallas_call x1, Pallas kernels, decoded(): pl.pallas_call(kernel, out_shape=jax.ShapeDtypeStruct((2 * frames, 4, 16,...  45.2 us
    unnamed x1, local copies, waits for them, and re-layouts  2.41 us

profile of v4, /device:TPU:1, one launch (start us, length us, event | category | flops | bytes accessed | tf_op | source)
XLA Modules:
  0.0 48.2 jit_solution(16227070760371955499)
XLA Ops:
  0.7 45.2 %shard_map.91 = f32[18,4,16,256]{3,2,1,0:T(8,128)} custom-call(s32[1]{0:T(128)S(6)} %copy.11.offsets, s32[16]{0:T(128)} %lengths.1, f32[9,16,512]{2,1,0:T(8,128)} %bitcast.7, f32[1,512]{1,0:T(1,128)} %bitcast.9, f32[1,512]{1,0:T(1,128)} %bitcast.10, f32[3,512,1024]{2,1,0:T(8,128)} %time_in.1, f32[1,1024]{1,0:T(1,128)} %bitcast.8, ...), custom_call_target="tpu_custom_call" | custom-call | tf_op jit(solution)/shard_map/pallas_call | solution.py:488
  45.8 2.4 %copy.12 = f32[1,1,18,4,16,256]{5,4,3,2,1,0:T(8,128)} copy(f32[1,1,18,4,16,256]{5,4,3,2,1,0:T(8,128)} %bitcast.6) | data formatting | bytes 2359296

commit v5 on v4

--- a/solution.py
+++ b/solution.py
@@ -230,12 +230,12 @@
     for kind in range(5):
         mark_copy(kind).start()
 
-    def start_near(half):
-        for group in range(groups):
-            for step in (1, 2, 3):
-                near_copy(step, half, group).start()
-
-    start_near(0)
+    def start_near(half, group):
+        for step in (1, 2, 3):
+            near_copy(step, half, group).start()
+
+    start_near(0, 0)
+    start_near(0, 1)
 
     length = lengths[grp]
     loads[0].wait()
@@ -254,7 +254,8 @@
     def _(step):
         sums_copy(step).start()
 
-    start_near(1)
+    for half, group in ((1, 0), (0, 2), (1, 1), (1, 2)):
+        start_near(half, group)
 
     kinds[0] = marks[...]
 
@@ -372,35 +373,35 @@
     swap_vertical(0)
     wait_near(0, 1)
     swap_vertical(1)
-    swap_part(FACING, 1)
     loads[2].wait()
 
     @pl.loop(0, 16)
     def _(piece):
         prepare_space(piece, space_raw, space)
 
+    wait_near(1, 0)
+    swap_other(0)
+    swap_part(FACING, 1)
+    start_norms()
+    core_vertical(0)
     wait_near(0, 2)
     swap_vertical(2)
-    swap_part(FACING, 2)
-    start_norms()
-    core_vertical(0)
-    wait_near(1, 0)
-    swap_other(0)
     core_vertical(1)
     send_vertical(0)
     core_part(FACING, 0)
     wait_near(1, 1)
     swap_other(1)
-    core_vertical(2)
+    swap_part(FACING, 2)
+    core_other(0)
     send_vertical(1)
     core_part(FACING, 1)
-    core_other(0)
+    send_sides(0)
     wait_near(1, 2)
     swap_other(2)
+    core_vertical(2)
+    finish(0)
     send_vertical(2)
-    send_sides(0)
     core_part(FACING, 2)
-    finish(0)
 
     @pl.loop(1, 16)
     def _(other):

time: 48.8 us -> 48.1 us (0.986)
  no operation moved by 1% of the time
where the time goes in v5:
time: 48.1 us; the launch traced here: 47.9 us
  Pallas kernels  44.9 us (93%)
  local copies, waits for them, and re-layouts  2.41 us (5%)
  between operations  0.66 us (1%)
    pallas_call x1, Pallas kernels, decoded(): pl.pallas_call(kernel, out_shape=jax.ShapeDtypeStruct((2 * frames, 4, 16,...  44.9 us
    unnamed x1, local copies, waits for them, and re-layouts  2.41 us

profile of v5, /device:TPU:1, one launch (start us, length us, event | category | flops | bytes accessed | tf_op | source)
XLA Modules:
  0.0 47.9 jit_solution(1094956598702181786)
XLA Ops:
  0.7 44.9 %shard_map.91 = f32[18,4,16,256]{3,2,1,0:T(8,128)} custom-call(s32[1]{0:T(128)S(6)} %copy.11.offsets, s32[16]{0:T(128)} %lengths.1, f32[9,16,512]{2,1,0:T(8,128)} %bitcast.7, f32[1,512]{1,0:T(1,128)} %bitcast.9, f32[1,512]{1,0:T(1,128)} %bitcast.10, f32[3,512,1024]{2,1,0:T(8,128)} %time_in.1, f32[1,1024]{1,0:T(1,128)} %bitcast.8, ...), custom_call_target="tpu_custom_call" | custom-call | tf_op jit(solution)/shard_map/pallas_call | solution.py:489
  45.5 2.4 %copy.12 = f32[1,1,18,4,16,256]{5,4,3,2,1,0:T(8,128)} copy(f32[1,1,18,4,16,256]{5,4,3,2,1,0:T(8,128)} %bitcast.6) | data formatting | bytes 2359296

commit v6 on v5

--- a/solution.py
+++ b/solution.py
@@ -231,7 +231,7 @@
         mark_copy(kind).start()
 
     def start_near(half, group):
-        for step in (1, 2, 3):
+        for step in (2, 1, 3):
             near_copy(step, half, group).start()
 
     start_near(0, 0)
@@ -363,27 +363,27 @@
 
     wait_near(0, 0)
     swap_part(FACING, 0)
-    loads[1].wait()
-
-    @pl.loop(0, 24)
-    def _(piece):
-        prepare_time(piece, time_raw, time)
-
     learn_marks()
     swap_vertical(0)
     wait_near(0, 1)
     swap_vertical(1)
-    loads[2].wait()
-
-    @pl.loop(0, 16)
+    loads[1].wait()
+
+    @pl.loop(0, 24)
     def _(piece):
-        prepare_space(piece, space_raw, space)
+        prepare_time(piece, time_raw, time)
 
     wait_near(1, 0)
     swap_other(0)
     swap_part(FACING, 1)
     start_norms()
     core_vertical(0)
+    loads[2].wait()
+
+    @pl.loop(0, 16)
+    def _(piece):
+        prepare_space(piece, space_raw, space)
+
     wait_near(0, 2)
     swap_vertical(2)
     core_vertical(1)
@@ -442,12 +442,11 @@
         yield
         send_sides(1)
         yield
-        yield
         core_other(2)
         yield
+        send_sides(2)
         finish(1)
         yield
-        send_sides(2)
         finish(2)
 
     work, moves = compute(), transfers()

time: 48.1 us -> 47.9 us (level)
  no operation moved by 1% of the time
where the time goes in v6:
time: 47.9 us; the launch traced here: 47.7 us
  Pallas kernels  44.7 us (93%)
  local copies, waits for them, and re-layouts  2.41 us (5%)
  between operations  0.66 us (1%)
    pallas_call x1, Pallas kernels, decoded(): pl.pallas_call(kernel, out_shape=jax.ShapeDtypeStruct((2 * frames, 4, 16,...  44.7 us
    unnamed x1, local copies, waits for them, and re-layouts  2.41 us

profile of v6, /device:TPU:1, one launch (start us, length us, event | category | flops | bytes accessed | tf_op | source)
XLA Modules:
  0.0 47.7 jit_solution(15441031998993326044)
XLA Ops:
  0.7 44.7 %shard_map.91 = f32[18,4,16,256]{3,2,1,0:T(8,128)} custom-call(s32[1]{0:T(128)S(6)} %copy.11.offsets, s32[16]{0:T(128)} %lengths.1, f32[9,16,512]{2,1,0:T(8,128)} %bitcast.7, f32[1,512]{1,0:T(1,128)} %bitcast.9, f32[1,512]{1,0:T(1,128)} %bitcast.10, f32[3,512,1024]{2,1,0:T(8,128)} %time_in.1, f32[1,1024]{1,0:T(1,128)} %bitcast.8, ...), custom_call_target="tpu_custom_call" | custom-call | tf_op jit(solution)/shard_map/pallas_call | solution.py:488
  45.3 2.4 %copy.12 = f32[1,1,18,4,16,256]{5,4,3,2,1,0:T(8,128)} copy(f32[1,1,18,4,16,256]{5,4,3,2,1,0:T(8,128)} %bitcast.6) | data formatting | bytes 2359296
